TPU v7x, 1024 devices: a whole 4x8x16 slice. The times are simulated.
1024 devices in a mesh: rep: 64 (over x, y, core), shard: 16 (over z).
Axes of the slice: x: 4, y: 8, z: 16, core: 2. Of those that a mesh axis runs over, the one named last changes fastest.
Arguments:
- tokens: bfloat16 [24576, 4096], P('rep'), may hold values from -70 to 70
- cotangent: bfloat16 [24576, 4096], P('rep', 'shard'), may hold values from -30 to 30
- moment_one: float32 [4096, 4096], P('rep', 'shard'), may hold values from -6 to 6
- moment_two: float32 [4096, 4096], P('rep', 'shard'), may hold values from 0.1 to 10
- master: float32 [4096, 4096], P('rep', 'shard'), may hold values from -0.09375 to 0.09375
Outputs:
- merged_grad: float32 [4096, 4096], P('rep', 'shard')
- new_moment_one: float32 [4096, 4096], P('rep', 'shard')
- new_moment_two: float32 [4096, 4096], P('rep', 'shard')
- new_master: float32 [4096, 4096], P('rep', 'shard')
- new_weights: bfloat16 [4096, 4096], P(None, 'shard')
All inputs are finite; a program needn't handle non-finite values.
Results may differ from a plain program's by a relative error of at most 0.0004.
Values may be sent and summed in bfloat16 or wider, within the bound.
A program may use at most 64 MiB of HBM per device.

v0:
```python
import jax
import jax.numpy as jnp
from jax import lax
from jax.sharding import PartitionSpec as P

STEP = 10


def partner(block, axis, distance):
    count = lax.axis_size(axis)
    route = []
    for low in range(count):
        high = low | 1 << distance
        if high != low and high < count:
            route += [(low, high), (high, low)]
    return lax.ppermute(block, axis, route)


def outer_grad(left, right):
    return lax.dot_general(
        left, right, (((0,), (0,)), ((), ())), preferred_element_type=jnp.float32
    )


def subtree_sums(partial_value, bit, levels):
    for upper in range(bit, levels):
        partial_value = partial_value + partner(partial_value, "rep", upper)
    return lax.psum(partial_value, "shard")


def combine(kept, other, mine, bit, levels):
    first = jnp.where(mine == 0, kept, other)
    second = jnp.where(mine == 0, other, kept)
    partial_value = jnp.stack(
        [jnp.sum(first * first), jnp.sum(second * second), jnp.sum(first * second)]
    )
    totals = subtree_sums(partial_value, bit, levels)
    coef_first = 1.0 - totals[2] / (2.0 * (totals[0] + 1e-06))
    coef_second = 1.0 - totals[2] / (2.0 * (totals[1] + 1e-06))
    return coef_first * first + coef_second * second


def body(tokens, cotangent, moment_one, moment_two, master):
    levels = lax.axis_size("rep").bit_length() - 1
    rank = lax.axis_index("rep")
    width = tokens.shape[1]
    top = levels - 1
    mine = rank >> top & 1
    half = width // 2
    gradient = outer_grad(tokens, cotangent)
    kept = lax.dynamic_slice_in_dim(gradient, mine * half, half, 0)
    sending = lax.dynamic_slice_in_dim(gradient, (1 - mine) * half, half, 0)
    other = partner(sending, "rep", top)
    segment = combine(kept, other, mine, top, levels)
    for level in range(1, levels):
        bit = top - level
        mine = rank >> bit & 1
        half = segment.shape[0] // 2
        kept = lax.dynamic_slice_in_dim(segment, mine * half, half, 0)
        sending = lax.dynamic_slice_in_dim(segment, (1 - mine) * half, half, 0)
        other = partner(sending, "rep", bit)
        segment = combine(kept, other, mine, bit, levels)
    new_one = 0.9 * moment_one + 0.1 * segment
    new_two = 0.999 * moment_two + 0.001 * segment * segment
    first_fix = 1.0 - 0.9**STEP
    second_fix = 1.0 - 0.999**STEP
    update = new_one / first_fix / (jnp.sqrt(new_two / second_fix) + 1e-08) + 0.1 * master
    new_master = master - 0.001 * update
    new_weights = lax.all_gather(new_master.astype(jnp.bfloat16), "rep", axis=0, tiled=True)
    return (segment, new_one, new_two, new_master, new_weights)


def solution(mesh):
    return jax.shard_map(
        body,
        mesh=mesh,
        in_specs=(
            P("rep", None),
            P("rep", "shard"),
            P("rep", "shard"),
            P("rep", "shard"),
            P("rep", "shard"),
        ),
        out_specs=(
            P("rep", "shard"),
            P("rep", "shard"),
            P("rep", "shard"),
            P("rep", "shard"),
            P(None, "shard"),
        ),
        check_vma=False,
    )
```

profile of v0, /device:TPU:1, one launch (start us, length us, event | category | flops | bytes accessed | tf_op | source)
XLA Modules:
  0.0 631.8 jit_solution(14481870633102305998)
XLA Ops:
  9.1 2.2 fusion.9
  13.8 5.5 collective-permute-start
  19.3 34.9 %collective-permute-done = f32[2048,256]{1,0:T(8,128)} collective-permute-done((f32[2048,256]{1,0:T(8,128)}, f32[2048,256]{1,0:T(8,128)}, u32[]{:S(2)}, u32[]{:S(2)}) %collective-permute-start) | collective-permute-done | bytes 2097184 | tf_op jit(solution)/shard_map/ppermute | solution.py:16
  54.2 5.4 multiply_reduce_fusion.2
  61.6 5.6 collective-permute-start.1
  70.2 46.0 %psum.42 = f32[3]{0:T(128)S(1)} all-reduce(f32[3]{0:T(128)S(1)} %fusion.17), channel_id=1, replica_groups=mesh['rep'=64,'shard'=16] {'shard'}, use_global_device_ids=true, to_apply=%region_3.4 | all-reduce | flops 3 | bytes 24 | tf_op jit(solution)/shard_map/psum | solution.py:28
  119.4 2.5 multiply_add_fusion
  124.3 3.1 collective-permute-start.2
  127.5 13.8 %collective-permute-done.2 = f32[1024,256]{1,0:T(8,128)} collective-permute-done((f32[1024,256]{1,0:T(8,128)}, f32[1024,256]{1,0:T(8,128)}, u32[]{:S(2)}, u32[]{:S(2)}) %collective-permute-start.2) | collective-permute-done | bytes 1048608 | tf_op jit(solution)/shard_map/ppermute | solution.py:16
  141.3 3.8 multiply_reduce_fusion.5
  147.1 3.1 collective-permute-start.3
  153.7 4.6 collective-permute-start.4
  161.5 20.3 %psum.43 = f32[3]{0:T(128)S(1)} all-reduce(f32[3]{0:T(128)S(1)} %fusion.22), channel_id=1, replica_groups=mesh['rep'=64,'shard'=16] {'shard'}, use_global_device_ids=true, to_apply=%region_7.8 | all-reduce | flops 3 | bytes 24 | tf_op jit(solution)/shard_map/psum | solution.py:28
  188.6 7.4 %collective-permute-start.5 = (f32[512,256]{1,0:T(8,128)}, f32[512,256]{1,0:T(8,128)}, u32[]{:S(2)}, u32[]{:S(2)}) collective-permute-start(f32[512,256]{1,0:T(8,128)} %constant_dynamic-slice_fusion.3), channel_id=1, source_target_pairs={{0,128},{128,0},{16,144},{144,16},{32,160},{160,32},{48,176},{176,... | collective-permute-start | bytes 1572872 | tf_op jit(solution)/shard_map/ppermute | solution.py:16
  196.0 8.7 %collective-permute-done.5 = f32[512,256]{1,0:T(8,128)} collective-permute-done((f32[512,256]{1,0:T(8,128)}, f32[512,256]{1,0:T(8,128)}, u32[]{:S(2)}, u32[]{:S(2)}) %collective-permute-start.5) | collective-permute-done | bytes 524320 | tf_op jit(solution)/shard_map/ppermute | solution.py:16
  204.7 2.9 multiply_reduce_fusion.8
  209.6 11.1 %collective-permute-start.6 = (f32[3]{0:T(128)S(1)}, f32[3]{0:T(128)S(1)}, u32[]{:S(2)}, u32[]{:S(2)}) collective-permute-start(f32[3]{0:T(128)S(1)} %pad_maximum_fusion.2), channel_id=1, source_target_pairs={{0,128},{128,0},{16,144},{144,16},{32,160},{160,32},{48,176},{176,... | collective-permute-start | bytes 44 | tf_op jit(solution)/shard_map/ppermute | solution.py:16
  224.8 3.1 collective-permute-start.7
  231.1 4.6 collective-permute-start.8
  236.9 22.3 %psum.44 = f32[3]{0:T(128)S(1)} all-reduce(f32[3]{0:T(128)S(1)} %add.209), channel_id=1, replica_groups=mesh['rep'=64,'shard'=16] {'shard'}, use_global_device_ids=true, to_apply=%region_11.12 | all-reduce | flops 3 | bytes 24 | tf_op jit(solution)/shard_map/psum | solution.py:28
  264.5 2.9 collective-permute-start.9
  267.4 8.1 %collective-permute-done.9 = f32[256,256]{1,0:T(8,128)} collective-permute-done((f32[256,256]{1,0:T(8,128)S(1)}, f32[256,256]{1,0:T(8,128)}, u32[]{:S(2)}, u32[]{:S(2)}) %collective-permute-start.9) | collective-permute-done | bytes 262176 | tf_op jit(solution)/shard_map/ppermute | solution.py:16
  275.4 2.5 multiply_reduce_fusion.11
  281.8 3.3 collective-permute-done.10
  287.1 7.3 %collective-permute-start.11 = (f32[3]{0:T(128)S(1)}, f32[3]{0:T(128)S(1)}, u32[]{:S(2)}, u32[]{:S(2)}) collective-permute-start(f32[3]{0:T(128)S(1)} %fusion.14), channel_id=1, source_target_pairs={{0,128},{128,0},{16,144},{144,16},{32,160},{160,32},{48,176},{176,... | collective-permute-start | bytes 44 | tf_op jit(solution)/shard_map/ppermute | solution.py:16
  297.3 2.8 collective-permute-start.12
  302.0 4.4 collective-permute-start.13
  307.8 20.3 %psum.45 = f32[3]{0:T(128)S(1)} all-reduce(f32[3]{0:T(128)S(1)} %add.218), channel_id=1, replica_groups=mesh['rep'=64,'shard'=16] {'shard'}, use_global_device_ids=true, to_apply=%region_15.16 | all-reduce | flops 3 | bytes 24 | tf_op jit(solution)/shard_map/psum | solution.py:28
  334.4 3.9 collective-permute-done.14
  338.3 2.2 multiply_reduce_fusion.14
  344.4 2.5 collective-permute-done.15
  348.9 2.8 collective-permute-start.16
  351.8 2.6 collective-permute-done.16
  356.4 6.8 %collective-permute-start.17 = (f32[3]{0:T(128)S(1)}, f32[3]{0:T(128)S(1)}, u32[]{:S(2)}, u32[]{:S(2)}) collective-permute-start(f32[3]{0:T(128)S(1)} %fusion.19), channel_id=1, source_target_pairs={{0,128},{128,0},{16,144},{144,16},{32,160},{160,32},{48,176},{176,... | collective-permute-start | bytes 44 | tf_op jit(solution)/shard_map/ppermute | solution.py:16
  364.6 2.4 collective-permute-start.18
  369.0 4.4 collective-permute-start.19
  374.7 21.0 %psum.46 = f32[3]{0:T(128)S(1)} all-reduce(f32[3]{0:T(128)S(1)} %add.228), channel_id=1, replica_groups=mesh['rep'=64,'shard'=16] {'shard'}, use_global_device_ids=true, to_apply=%region_19.20 | all-reduce | flops 3 | bytes 24 | tf_op jit(solution)/shard_map/psum | solution.py:28
  399.8 57.6 %collective-permute-start.20 = (f32[64,256]{1,0:T(8,128)S(1)}, f32[64,256]{1,0:T(8,128)S(1)}, u32[]{:S(2)}, u32[]{:S(2)}) collective-permute-start(f32[64,256]{1,0:T(8,128)S(1)} %constant_dynamic-slice_fusion), channel_id=1, source_target_pairs={{0,16},{16,0},{32,48},{48,32},{64,80},{80,64},{96,112},{112,96},{1... | collective-permute-start | bytes 196616 | tf_op jit(solution)/shard_map/ppermute | solution.py:16
  460.9 2.3 collective-permute-start.21
  466.0 2.2 collective-permute-start.22
  468.2 2.1 collective-permute-done.22
  472.3 3.3 collective-permute-start.23
  477.5 7.5 %collective-permute-start.24 = (f32[3]{0:T(128)S(1)}, f32[3]{0:T(128)S(1)}, u32[]{:S(2)}, u32[]{:S(2)}) collective-permute-start(f32[3]{0:T(128)S(1)} %add.236), channel_id=1, source_target_pairs={{0,128},{128,0},{16,144},{144,16},{32,160},{160,32},{48,176},{176,... | collective-permute-start | bytes 44 | tf_op jit(solution)/shard_map/ppermute | solution.py:16
  485.9 3.1 collective-permute-start.25
  490.2 4.6 collective-permute-start.26
  495.9 20.3 %psum.47 = f32[3]{0:T(128)S(1)} all-reduce(f32[3]{0:T(128)S(1)} %add.239), channel_id=1, replica_groups=mesh['rep'=64,'shard'=16] {'shard'}, use_global_device_ids=true, to_apply=%region_23.24 | all-reduce | flops 3 | bytes 24 | tf_op jit(solution)/shard_map/psum | solution.py:28
  521.1 100.8 %all-gather.2.cloned.1.call-done = bf16[4096,256]{1,0:T(8,128)(2,1)} async-done(((bf16[64,256]{1,0:T(8,128)(2,1)}), bf16[4096,256]{1,0:T(8,128)(2,1)}) %all-gather.2.cloned.1.call-update) | async-done | bytes 2097168 | tf_op jit(solution)/shard_map/all_gather | solution.py:69
  621.9 3.0 copy.11
  (78 shorter events, 83.7 us)
Async XLA Ops:
  7.2 1.9 copy-start
  7.2 614.7 %all-gather.2.cloned.1.call-start = ((), (), s32[]{:S(2)}) async-start(), calls=%async_computation | async-start | bytes 2129920 | tf_op jit(solution)/shard_map/all_gather | solution.py:69
  11.3 2.6 copy-start.1
  13.8 40.4 %collective-permute-start = (f32[2048,256]{1,0:T(8,128)}, f32[2048,256]{1,0:T(8,128)}, u32[]{:S(2)}, u32[]{:S(2)}) collective-permute-start(f32[2048,256]{1,0:T(8,128)} %constant_dynamic-slice_fusion.5), channel_id=1, source_target_pairs={{0,512},{512,0},{16,528},{528,16},{32,544},{544,32},{48,560},{560,... | collective-permute-start | bytes 6291464 | tf_op jit(solution)/shard_map/ppermute | solution.py:16
  61.6 6.5 %collective-permute-start.1 = (f32[3]{0:T(128)S(1)}, f32[3]{0:T(128)S(1)}, u32[]{:S(2)}, u32[]{:S(2)}) collective-permute-start(f32[3]{0:T(128)S(1)} %pad_maximum_fusion), channel_id=1, source_target_pairs={{0,512},{512,0},{16,528},{528,16},{32,544},{544,32},{48,560},{560,... | collective-permute-start | bytes 44 | tf_op jit(solution)/shard_map/ppermute | solution.py:16
  121.9 1.3 copy-start.2
  124.3 17.0 %collective-permute-start.2 = (f32[1024,256]{1,0:T(8,128)}, f32[1024,256]{1,0:T(8,128)}, u32[]{:S(2)}, u32[]{:S(2)}) collective-permute-start(f32[1024,256]{1,0:T(8,128)} %constant_dynamic-slice_fusion.4), channel_id=1, source_target_pairs={{0,256},{256,0},{16,272},{272,16},{32,288},{288,32},{48,304},{304,... | collective-permute-start | bytes 3145736 | tf_op jit(solution)/shard_map/ppermute | solution.py:16
  147.1 4.6 collective-permute-start.3
  153.7 5.8 collective-permute-start.4
  186.7 1.0 copy-start.3
  188.6 16.1 %collective-permute-start.5 = (f32[512,256]{1,0:T(8,128)}, f32[512,256]{1,0:T(8,128)}, u32[]{:S(2)}, u32[]{:S(2)}) collective-permute-start(f32[512,256]{1,0:T(8,128)} %constant_dynamic-slice_fusion.3), channel_id=1, source_target_pairs={{0,128},{128,0},{16,144},{144,16},{32,160},{160,32},{48,176},{176,... | collective-permute-start | bytes 1572872 | tf_op jit(solution)/shard_map/ppermute | solution.py:16
  209.6 13.2 %collective-permute-start.6 = (f32[3]{0:T(128)S(1)}, f32[3]{0:T(128)S(1)}, u32[]{:S(2)}, u32[]{:S(2)}) collective-permute-start(f32[3]{0:T(128)S(1)} %pad_maximum_fusion.2), channel_id=1, source_target_pairs={{0,128},{128,0},{16,144},{144,16},{32,160},{160,32},{48,176},{176,... | collective-permute-start | bytes 44 | tf_op jit(solution)/shard_map/ppermute | solution.py:16
  224.8 4.3 collective-permute-start.7
  231.1 5.8 collective-permute-start.8
  263.7 0.8 copy-start.4
  264.5 10.9 %collective-permute-start.9 = (f32[256,256]{1,0:T(8,128)S(1)}, f32[256,256]{1,0:T(8,128)}, u32[]{:S(2)}, u32[]{:S(2)}) collective-permute-start(f32[256,256]{1,0:T(8,128)S(1)} %constant_dynamic-slice_fusion.2), channel_id=1, source_target_pairs={{0,64},{64,0},{16,80},{80,16},{32,96},{96,32},{48,112},{112,48},{1... | collective-permute-start | bytes 786440 | tf_op jit(solution)/shard_map/ppermute | solution.py:16
  279.9 5.2 collective-permute-start.10
  287.1 8.2 %collective-permute-start.11 = (f32[3]{0:T(128)S(1)}, f32[3]{0:T(128)S(1)}, u32[]{:S(2)}, u32[]{:S(2)}) collective-permute-start(f32[3]{0:T(128)S(1)} %fusion.14), channel_id=1, source_target_pairs={{0,128},{128,0},{16,144},{144,16},{32,160},{160,32},{48,176},{176,... | collective-permute-start | bytes 44 | tf_op jit(solution)/shard_map/ppermute | solution.py:16
  297.3 4.7 collective-permute-start.12
  302.0 5.8 collective-permute-start.13
  332.4 5.8 collective-permute-start.14
  342.5 4.4 collective-permute-start.15
  348.9 5.5 collective-permute-start.16
  356.4 8.2 %collective-permute-start.17 = (f32[3]{0:T(128)S(1)}, f32[3]{0:T(128)S(1)}, u32[]{:S(2)}, u32[]{:S(2)}) collective-permute-start(f32[3]{0:T(128)S(1)} %fusion.19), channel_id=1, source_target_pairs={{0,128},{128,0},{16,144},{144,16},{32,160},{160,32},{48,176},{176,... | collective-permute-start | bytes 44 | tf_op jit(solution)/shard_map/ppermute | solution.py:16
  364.6 4.4 collective-permute-start.18
  369.0 5.8 collective-permute-start.19
  399.8 58.5 %collective-permute-start.20 = (f32[64,256]{1,0:T(8,128)S(1)}, f32[64,256]{1,0:T(8,128)S(1)}, u32[]{:S(2)}, u32[]{:S(2)}) collective-permute-start(f32[64,256]{1,0:T(8,128)S(1)} %constant_dynamic-slice_fusion), channel_id=1, source_target_pairs={{0,16},{16,0},{32,48},{48,32},{64,80},{80,64},{96,112},{112,96},{1... | collective-permute-start | bytes 196616 | tf_op jit(solution)/shard_map/ppermute | solution.py:16
  460.9 3.1 collective-permute-start.21
  466.0 4.3 collective-permute-start.22
  472.3 5.2 collective-permute-start.23
  477.5 8.4 %collective-permute-start.24 = (f32[3]{0:T(128)S(1)}, f32[3]{0:T(128)S(1)}, u32[]{:S(2)}, u32[]{:S(2)}) collective-permute-start(f32[3]{0:T(128)S(1)} %add.236), channel_id=1, source_target_pairs={{0,128},{128,0},{16,144},{144,16},{32,160},{160,32},{48,176},{176,... | collective-permute-start | bytes 44 | tf_op jit(solution)/shard_map/ppermute | solution.py:16
  485.9 4.3 collective-permute-start.25
  490.2 5.8 collective-permute-start.26
Sparse Core Ops, SparseCore 0:
  521.2 100.6 all-gather.1
where the time goes:
time: 634 us; the launch traced here: 632 us
  waiting for transfers between devices  204 us (32%)
  starting transfers between devices  168 us (26%)
  blocking collectives  150 us (24%)
  other arithmetic  60.7 us (10%)
  between operations  30.1 us (5%)
  local copies, waits for them, and re-layouts  16 us (3%)
    ppermute x27, starting transfers between devices, partner(): return lax.ppermute(block, axis, route)  168 us
    psum x6, blocking collectives, subtree_sums(): return lax.psum(partial_value, 'shard')  150 us
    ppermute x27, waiting for transfers between devices, partner(): return lax.ppermute(block, axis, route)  103 us
    all_gather x1, waiting for transfers between devices, body(): lax.all_gather(new_master.astype(jnp.bfloat16), 'rep', axis=0, tiled=True)  101 us
    add x21, other arithmetic, subtree_sums(): partial_value = partial_value + partner(partial_value, 'rep', upper)  22.2 us
    reduce_sum x6, other arithmetic, combine(): jnp.sum(first * first)  17.4 us
  transfers between devices with their start and end apart: 28, of which 28 were waited for; matrix products, arithmetic and copies ran while one was open for 0% of the time, Pallas kernels for 0%

commit v1 on v0

v1 whole, which is shorter than its diff:
```python
import functools

import jax
import jax.numpy as jnp
from jax import lax
from jax.experimental import pallas as pl
from jax.experimental.pallas import tpu as pltpu
from jax.sharding import PartitionSpec as P

STEP = 10
CORES = 2
CHIPS_Y = 8
TILES = 4
HEAD = 16
TOP = 2.0**15.75
TINY = 2.0**-126
MESH = pl.DeviceIdType.MESH


def encode(block, ref):
    rows = block.shape[0]
    for half in range(2):
        part = block[:, half * 128 : half * 128 + 128]
        peak = jnp.max(jnp.abs(part), axis=0, keepdims=True)
        scale = (peak * 1.01 + 1e-30).astype(jnp.bfloat16)
        unit = part * (TOP / scale.astype(jnp.float32))
        power = unit * unit
        power = power * power
        power = power * power
        power = jnp.where(part < 0.0, -power, power)
        ref[half * rows : half * rows + rows, :] = power.astype(jnp.bfloat16)
        ref[2 * rows + half * 8 : 2 * rows + half * 8 + 8, :] = jnp.broadcast_to(
            scale.astype(jnp.float32), (8, 128)
        ).astype(jnp.bfloat16)


def decode(ref, rows, half):
    scale = ref[2 * rows : 2 * rows + HEAD, :].astype(jnp.float32)
    scale = scale[half * 8 : half * 8 + 1, :] * (1.0 / TOP)
    coded = ref[half * rows : half * rows + rows, :].astype(jnp.float32)
    size = lax.rsqrt(lax.rsqrt(jnp.maximum(jnp.abs(coded), TINY)))
    value = size * lax.rsqrt(size) * scale
    return jnp.where(coded < 0.0, -value, value)


def pair_sums(data, sums, n, rows, first):
    width = max(n, 8)
    block = min(n, 4)
    for qb in range(0, n, block):
        for sb in range(qb, n, block):
            pairs = [
                (q, s)
                for q in range(qb, qb + block)
                for s in range(sb, sb + block)
                if q <= s
            ]

            def step(i, totals):
                at = pl.ds(pl.multiple_of(i * 8, 8), 8)
                out = list(totals)
                for half in range(2):
                    lanes = pl.ds(half * 128, 128)
                    item = {k: data[k, at, lanes] for k in {k for p in pairs for k in p}}
                    out = [o + item[q] * item[s] for o, (q, s) in zip(out, pairs)]
                return tuple(out)

            zero = jnp.zeros((8, 128), jnp.float32)
            totals = lax.fori_loop(0, rows // 8, step, (zero,) * len(pairs), unroll=2)
            for total, (q, s) in zip(totals, pairs):
                for a, b in {(q, s), (s, q)}:
                    at = (b * width + a) * 8
                    if first:
                        sums[at : at + 8, :] = total
                    else:
                        sums[at : at + 8, :] += total


def packing(n):
    per_row = min(n, 128 // n)
    return per_row, n // per_row


def pack(sums, n):
    width = max(n, 8)
    per_row, count = packing(n)
    sub = lax.broadcasted_iota(jnp.int32, (width, 128), 0)
    lane = lax.broadcasted_iota(jnp.int32, (width, 128), 1)
    place = (sub % per_row) * n
    gram = jnp.zeros((width, 128), jnp.float32)
    for s in range(n):
        part = sums[pl.ds(s * width * 8, width, 8), :]
        for i in range(1, 8):
            part = part + sums[pl.ds(s * width * 8 + i, width, 8), :]
        total = jnp.sum(part, axis=1, keepdims=True)
        gram = gram + jnp.where((lane == place + s) & (sub < n), total, 0.0)
    if count == 1:
        return jnp.sum(gram, axis=0, keepdims=True)
    return jnp.concatenate(
        [
            jnp.sum(gram[k * per_row : (k + 1) * per_row, :], axis=0, keepdims=True)
            for k in range(count)
        ],
        axis=0,
    )


def unpack(packed, n):
    width = max(n, 8)
    per_row, count = packing(n)
    each = width // count
    pieces = []
    for k in range(count):
        row = jnp.broadcast_to(packed[k : k + 1, :], (each, 128))
        sub = lax.broadcasted_iota(jnp.int32, (each, 128), 0)
        piece = row
        for q in range(1, per_row):
            piece = jnp.where(sub == q, pltpu.roll(row, 128 - q * n, 1), piece)
        pieces.append(piece)
    gram = pieces[0] if count == 1 else jnp.concatenate(pieces, axis=0)
    sub = lax.broadcasted_iota(jnp.int32, (width, 128), 0)
    lane = lax.broadcasted_iota(jnp.int32, (width, 128), 1)
    return jnp.where((lane < n) & (sub < n), gram, 0.0)


def swap(value, bit, axis):
    index = lax.broadcasted_iota(jnp.int32, value.shape, axis)
    size = value.shape[axis]
    up = pltpu.roll(value, bit, axis)
    down = pltpu.roll(value, size - bit, axis)
    return jnp.where((index // bit) % 2 == 1, up, down)


def adasum_weights(gram, n):
    width = gram.shape[0]
    sub = lax.broadcasted_iota(jnp.int32, (width, 128), 0)
    lane = lax.broadcasted_iota(jnp.int32, (width, 128), 1)
    weight = jnp.ones((width, 128), jnp.float32)
    bit = n // 2
    while bit:
        own = jnp.where(lane == sub, gram, 0.0)
        other = jnp.where(lane == jnp.where((sub // bit) % 2 == 1, sub - bit, sub + bit), gram, 0.0)
        down = 1.0 - jnp.sum(other, axis=1, keepdims=True) / (
            2.0 * (jnp.sum(own, axis=1, keepdims=True) + 1e-06)
        )
        down = jnp.broadcast_to(down, (width, 128))
        weight = weight * down
        if bit > 1:
            across = 1.0 - jnp.sum(other, axis=0, keepdims=True) / (
                2.0 * (jnp.sum(own, axis=0, keepdims=True) + 1e-06)
            )
            across = jnp.broadcast_to(across, (width, 128))
            scaled = across * gram
            scaled = scaled + swap(scaled, bit, 1)
            scaled = down * scaled
            gram = scaled + swap(scaled, bit, 0)
        bit //= 2
    return weight


def kernel(
    chips_x, shards, tokens, cotangent, moment_one, moment_two, master,
    out_grad, out_one, out_two, out_master, out_weights,
    x_send, x_recv, terms, x_sums, y_send, y_recv, parts, y_sums,
    z_one, x_one, z_two, x_two, y_two,
    x_ssem, x_rsem, y_ssem, y_rsem,
    z1_ssem, z1_rsem, x1_ssem, x1_rsem, z2_ssem, z2_rsem, x2_ssem, x2_rsem, y2_ssem, y2_rsem,
    wy_ssem, wy_rsem, wx_ssem, wx_rsem, wc_ssem, wc_rsem,
):
    rank, z = lax.axis_index("rep"), lax.axis_index("shard")
    peers = out_weights.shape[1] * CORES
    chips_y = out_weights.shape[1]
    x, place = rank // peers, rank % peers
    y, core = place // CORES, place % CORES
    rows_x = terms.shape[1]
    rows = out_grad.shape[0]
    tile = rows_x // TILES

    def remote(src, dst, ssem, rsem, device):
        return pltpu.make_async_remote_copy(
            src_ref=src, dst_ref=dst, send_sem=ssem, recv_sem=rsem,
            device_id=device, device_id_type=MESH,
        )

    def at_x(i):
        return (i * peers + place, z)

    def at_place(i):
        return (x * peers + i, z)

    def at_z(i):
        return (rank, i)

    barrier = pltpu.get_barrier_semaphore()
    for me, count, device in ((x, chips_x, at_x), (place, peers, at_place), (z, shards, at_z)):

        def greet(d, _, me=me, count=count, device=device):
            pl.semaphore_signal(
                barrier, inc=1, device_id=device((me + d) % count), device_id_type=MESH
            )
            return 0

        lax.fori_loop(1, count, greet, 0)

    def gradient(owner, t):
        at = pl.multiple_of(owner * rows_x + t * tile, tile)
        return lax.dot_general(
            tokens[:, pl.ds(at, tile)], cotangent[...], (((0,), (0,)), ((), ())),
            preferred_element_type=jnp.float32,
        )

    def x_copy(d, t):
        to = (x + d) % chips_x
        return remote(
            x_send.at[d - 1, t], x_recv.at[x, t], x_ssem.at[d - 1, t], x_rsem.at[x, t], at_x(to)
        )

    for t in range(TILES):
        for d in range(1, chips_x):
            encode(gradient((x + d) % chips_x, t), x_send.at[d - 1, t])
            if t == 0 and d == 1:
                pl.semaphore_wait(barrier, chips_x + peers + shards - 3)
            x_copy(d, t).start()
    for t in range(TILES):
        terms[x, t * tile : t * tile + tile, :] = gradient(x, t)

    for t in range(TILES):
        for d in range(1, chips_x):
            source = (x + d) % chips_x
            remote(
                x_send.at[d - 1, t], x_recv.at[source, t],
                x_ssem.at[d - 1, t], x_rsem.at[source, t], at_x(source),
            ).wait_recv()
            for half in range(2):
                terms[source, t * tile : t * tile + tile, half * 128 : half * 128 + 128] = decode(
                    x_recv.at[source, t], tile, half
                )
        pair_sums(terms.at[:, pl.ds(t * tile, tile), :], x_sums, chips_x, tile, t == 0)

    def total(value, slots, ssem, rsem, me, count, device):
        slots[me] = value

        def copy(i, to):
            return remote(slots.at[i], slots.at[i], ssem.at[to], rsem.at[i], device(to))

        def send(d, _):
            copy(me, (me + d) % count).start()
            return 0

        def wait(d, _):
            other = (me + d) % count
            copy(other, other).wait_recv()
            return 0

        def done(d, _):
            copy(me, (me + d) % count).wait_send()
            return 0

        lax.fori_loop(1, count, send, 0)
        lax.fori_loop(1, count, wait, 0)
        result = slots[0]
        for i in range(1, count):
            result = result + slots[i]
        lax.fori_loop(1, count, done, 0)
        return result

    gram = pack(x_sums, chips_x)
    gram = total(gram, z_one, z1_ssem, z1_rsem, z, shards, at_z)
    gram = total(gram, x_one, x1_ssem, x1_rsem, x, chips_x, at_x)
    weight = adasum_weights(unpack(gram, chips_x), chips_x)

    def combine(ref, at, size, weight, n, half):
        lanes = pl.ds(half * 128, 128)
        value = weight[0:1, :] * ref[0, pl.ds(at, size), lanes]
        for k in range(1, n):
            value = value + weight[k : k + 1, :] * ref[k, pl.ds(at, size), lanes]
        return value

    def y_copy(to):
        return remote(
            y_send.at[to], y_recv.at[place], y_ssem.at[to], y_rsem.at[place], at_place(to)
        )

    def y_block(to):
        at = pl.multiple_of(to * rows, rows)
        return jnp.concatenate(
            [combine(terms, at, rows, weight, chips_x, half) for half in range(2)], axis=1
        )

    def y_start(d, _):
        to = (place + d) % peers
        encode(y_block(to), y_send.at[to])
        y_copy(to).start()
        return 0

    lax.fori_loop(1, peers, y_start, 0)
    parts[place] = y_block(place)

    def y_wait(d, _):
        source = (place + d) % peers
        remote(
            y_send.at[source], y_recv.at[source],
            y_ssem.at[source], y_rsem.at[source], at_place(source),
        ).wait_recv()
        for half in range(2):
            parts[source, :, pl.ds(half * 128, 128)] = decode(y_recv.at[source], rows, half)
        return 0

    lax.fori_loop(1, peers, y_wait, 0)
    pair_sums(parts, y_sums, peers, rows, True)
    gram = pack(y_sums, peers)
    gram = total(gram, z_two, z2_ssem, z2_rsem, z, shards, at_z)
    gram = total(gram, x_two, x2_ssem, x2_rsem, x, chips_x, at_x)
    gram = total(gram, y_two, y2_ssem, y2_rsem, place, peers, at_place)
    weight = adasum_weights(unpack(gram, peers), peers)

    for half in range(2):
        lanes = pl.ds(half * 128, 128)
        merged = combine(parts, 0, rows, weight, peers, half)
        new_one = 0.9 * moment_one[:, lanes] + 0.1 * merged
        new_two = 0.999 * moment_two[:, lanes] + 0.001 * merged * merged
        first_fix = 1.0 - 0.9**STEP
        second_fix = 1.0 - 0.999**STEP
        old = master[:, lanes]
        update = new_one / first_fix / (jnp.sqrt(new_two / second_fix) + 1e-08) + 0.1 * old
        new_master = old - 0.001 * update
        out_grad[:, lanes] = merged
        out_one[:, lanes] = new_one
        out_two[:, lanes] = new_two
        out_master[:, lanes] = new_master
        out_weights[x, y, core, :, lanes] = new_master.astype(jnp.bfloat16)

    def wy_copy(source, to):
        block = out_weights.at[x, source, core]
        return remote(
            block, block, wy_ssem.at[to], wy_rsem.at[source], (x * peers + to * CORES + core, z)
        )

    def wx_copy(source, to):
        block = out_weights.at[source, :, core]
        return remote(block, block, wx_ssem.at[to], wx_rsem.at[source], at_x(to))

    def wc_copy(source, which):
        block = out_weights.at[source, :, which]
        return remote(
            block, block, wc_ssem.at[source], wc_rsem.at[source], at_place(y * CORES + 1 - core)
        )

    for d in range(1, chips_y):
        wy_copy(y, (y + d) % chips_y).start()
    for d in range(1, chips_y):
        wy_copy((y + d) % chips_y, (y + d) % chips_y).wait_recv()
    for d in range(1, chips_x):
        wx_copy(x, (x + d) % chips_x).start()
    wc_copy(x, core).start()
    for d in range(1, chips_x):
        source = (x + d) % chips_x
        wx_copy(source, source).wait_recv()
        wc_copy(source, core).start()
    for i in range(chips_x):
        wc_copy(i, 1 - core).wait_recv()
    for i in range(chips_x):
        wc_copy(i, core).wait_send()
    for d in range(1, chips_x):
        wx_copy(x, (x + d) % chips_x).wait_send()
    for d in range(1, chips_y):
        wy_copy(y, (y + d) % chips_y).wait_send()
    for d in range(1, chips_x):
        for t in range(TILES):
            x_copy(d, t).wait_send()

    def y_done(d, _):
        y_copy((place + d) % peers).wait_send()
        return 0

    lax.fori_loop(1, peers, y_done, 0)


def body(chips_y, tokens, cotangent, moment_one, moment_two, master):
    shards = lax.axis_size("shard")
    ranks = lax.axis_size("rep")
    peers = chips_y * CORES
    chips_x = ranks // peers
    depth, wide = tokens.shape[1], cotangent.shape[1]
    rows_x, rows = depth // chips_x, depth // ranks
    tile = rows_x // TILES
    coded = jnp.bfloat16
    f32 = jnp.float32
    one = (packing(chips_x)[1], 128)
    two = (packing(peers)[1], 128)
    dma = pltpu.SemaphoreType.DMA
    block = jax.ShapeDtypeStruct((rows, wide), f32)
    vmem = pl.BlockSpec(memory_space=pltpu.VMEM)
    outs = pl.pallas_call(
        functools.partial(kernel, chips_x, shards),
        out_shape=(
            block, block, block, block,
            jax.ShapeDtypeStruct((chips_x, chips_y, CORES, rows, wide), jnp.bfloat16),
        ),
        in_specs=[vmem] * 5,
        out_specs=(vmem,) * 5,
        scratch_shapes=[
            pltpu.VMEM((chips_x - 1, TILES, 2 * tile + HEAD, 128), coded),
            pltpu.VMEM((chips_x, TILES, 2 * tile + HEAD, 128), coded),
            pltpu.VMEM((chips_x, rows_x, wide), f32),
            pltpu.VMEM((chips_x * max(chips_x, 8) * 8, 128), f32),
            pltpu.VMEM((peers, 2 * rows + HEAD, 128), coded),
            pltpu.VMEM((peers, 2 * rows + HEAD, 128), coded),
            pltpu.VMEM((peers, rows, wide), f32),
            pltpu.VMEM((peers * max(peers, 8) * 8, 128), f32),
            pltpu.VMEM((shards,) + one, f32),
            pltpu.VMEM((chips_x,) + one, f32),
            pltpu.VMEM((shards,) + two, f32),
            pltpu.VMEM((chips_x,) + two, f32),
            pltpu.VMEM((peers,) + two, f32),
            dma((chips_x - 1, TILES)), dma((chips_x, TILES)),
            dma((peers,)), dma((peers,)),
            dma((shards,)), dma((shards,)),
            dma((chips_x,)), dma((chips_x,)),
            dma((shards,)), dma((shards,)),
            dma((chips_x,)), dma((chips_x,)),
            dma((peers,)), dma((peers,)),
            dma((chips_y,)), dma((chips_y,)),
            dma((chips_x,)), dma((chips_x,)),
            dma((chips_x,)), dma((chips_x,)),
        ],
        compiler_params=pltpu.CompilerParams(
            collective_id=0, has_side_effects=True, vmem_limit_bytes=48 * 1024 * 1024
        ),
        cost_estimate=pl.CostEstimate(
            flops=2 * tokens.shape[0] * depth * wide,
            bytes_accessed=6 * 1024 * 1024,
            transcendentals=0,
        ),
    )(tokens, cotangent, moment_one, moment_two, master)
    return outs[:4] + (outs[4].reshape(depth, wide),)


def solution(mesh, chips_y=CHIPS_Y):
    return jax.shard_map(
        functools.partial(body, chips_y),
        mesh=mesh,
        in_specs=(
            P("rep", None),
            P("rep", "shard"),
            P("rep", "shard"),
            P("rep", "shard"),
            P("rep", "shard"),
        ),
        out_specs=(
            P("rep", "shard"),
            P("rep", "shard"),
            P("rep", "shard"),
            P("rep", "shard"),
            P(None, "shard"),
        ),
        check_vma=False,
    )
```

time: 634 us -> 129 us (0.20)
  waiting for transfers between devices: 204 us -> 0 us
  starting transfers between devices: 168 us -> 0 us
  blocking collectives: 150 us -> 0 us
  Pallas kernels: 0 us -> 119 us
  other arithmetic: 60.7 us -> 0 us
  between operations: 30.1 us -> 0.66 us
  local copies, waits for them, and re-layouts: 16 us -> 9.16 us
    ppermute x27 -> x0, starting transfers between devices: 168 us -> none  [partner(): return lax.ppermute(block, axis, route)]
    psum x6 -> x0, blocking collectives: 150 us -> none  [subtree_sums(): return lax.psum(partial_value, 'shard')]
    pallas_call x0 -> x1, Pallas kernels: none -> 119 us  [body(): pl.pallas_call(functools.partial(kernel, chips_x, shards), out_shape=(blo...]
    ppermute x27 -> x0, waiting for transfers between devices: 103 us -> none  [partner(): return lax.ppermute(block, axis, route)]
    all_gather x1 -> x0, waiting for transfers between devices: 101 us -> none  [body(): lax.all_gather(new_master.astype(jnp.bfloat16), 'rep', axis=0, tiled=True)]
    add x26 -> x0, other arithmetic: 29.6 us -> none  [the longest x21 22.2 us: subtree_sums(): partial_value = partial_value + partner(partial_value, 'rep', upper)]
    reduce_sum x6 -> x0, other arithmetic: 17.4 us -> none  [combine(): jnp.sum(first * first)]
    another operation x6 -> x0, other arithmetic: 12.1 us -> none  [combine(): jnp.stack([jnp.sum(first * first), jnp.sum(second * second), jnp.sum(firs...]
  transfers between devices with their start and end apart: 28 -> 0, of which waited for: 28 -> 0; matrix products, arithmetic and copies ran while one was open for 0% -> 0% of each run, Pallas kernels for 0% -> 0%
where the time goes in v1:
time: 129 us; the launch traced here: 128 us
  Pallas kernels  119 us (92%)
  local copies, waits for them, and re-layouts  9.16 us (7%)
    pallas_call x1, Pallas kernels, body(): pl.pallas_call(functools.partial(kernel, chips_x, shards), out_shape=(blo...  119 us
    unnamed x15, local copies, waits for them, and re-layouts  9.16 us

profile of v1, /device:TPU:1, one launch (start us, length us, event | category | flops | bytes accessed | tf_op | source)
XLA Modules:
  0.0 128.3 jit_solution(12581706183367419418)
XLA Ops:
  0.6 0.0 copy-start
  0.6 1.9 %copy-done = bf16[384,4096]{1,0:T(8,128)(2,1)S(1)} copy-done((bf16[384,4096]{1,0:T(8,128)(2,1)S(1)}, bf16[384,4096]{1,0:T(8,128)(2,1)}, u32[]{:S(2)}) %copy-start) | copy-done | bytes 3145752
  2.5 0.0 copy-start.1
  2.5 0.9 copy-done.1
  3.5 0.0 copy-start.2
  3.5 0.8 copy-done.2
  4.3 0.0 copy-start.3
  4.3 0.8 copy-done.3
  5.1 0.0 copy-start.4
  5.1 0.8 copy-done.4
  6.0 118.5 %shard_map.92 = (f32[64,256]{1,0:T(8,128)S(1)}, f32[64,256]{1,0:T(8,128)S(1)}, f32[64,256]{1,0:T(8,128)S(1)}, f32[64,256]{1,0:T(8,128)S(1)}, bf16[4,8,2,64,256]{4,3,2,1,0:T(8,128)(2,1)S(1)}) custom-call(bf16[384,4096]{1,0:T(8,128)(2,1)S(1)} %copy-done, bf16[384,256]{1,0:T(8,128)(2,1)S(1)} %copy-done.1, f32[64,256]{1,0:T(8,128)S(1)} %copy-done.2, ...), custom_call_target="tpu_custom_call" | custom-call | flops 805306368 | bytes 6291456 | tf_op jit(solution)/shard_map/pallas_call | solution.py:393
  124.5 0.6 copy.15
  125.1 0.6 copy.16
  125.8 0.6 copy.17
  126.4 0.6 copy.18
  127.0 1.3 %copy.19 = bf16[4096,256]{1,0:T(8,128)(2,1)} copy(bf16[4096,256]{1,0:T(8,128)(2,1)S(1)} %bitcast.1) | data formatting | bytes 4194304
Async XLA Ops:
  0.6 1.9 %copy-start = (bf16[384,4096]{1,0:T(8,128)(2,1)S(1)}, bf16[384,4096]{1,0:T(8,128)(2,1)}, u32[]{:S(2)}) copy-start(bf16[384,4096]{1,0:T(8,128)(2,1)} %tokens.1) | copy-start | bytes 9437188
  2.5 0.9 copy-start.1
  3.5 0.8 copy-start.2
  4.3 0.8 copy-start.3
  5.1 0.8 copy-start.4

commit v2 on v1

--- a/solution.py
+++ b/solution.py
@@ -158,21 +158,22 @@
 
 
 def kernel(
-    chips_x, shards, tokens, cotangent, moment_one, moment_two, master,
-    out_grad, out_one, out_two, out_master, out_weights,
+    chips_x, shards, tokens_in, cotangent_in, one_in, two_in, master_in,
+    out_states, out_weights,
+    tokens, cotangent, states, in_sem, side_sem,
     x_send, x_recv, terms, x_sums, y_send, y_recv, parts, y_sums,
     z_one, x_one, z_two, x_two, y_two,
     x_ssem, x_rsem, y_ssem, y_rsem,
     z1_ssem, z1_rsem, x1_ssem, x1_rsem, z2_ssem, z2_rsem, x2_ssem, x2_rsem, y2_ssem, y2_rsem,
-    wy_ssem, wy_rsem, wx_ssem, wx_rsem, wc_ssem, wc_rsem,
+    wa_ssem, wa_rsem, wb_ssem, wb_rsem, wc_ssem, wc_rsem,
 ):
     rank, z = lax.axis_index("rep"), lax.axis_index("shard")
     peers = out_weights.shape[1] * CORES
     chips_y = out_weights.shape[1]
-    x, place = rank // peers, rank % peers
-    y, core = place // CORES, place % CORES
+    x, place = lax.div(rank, peers), lax.rem(rank, peers)
+    y, core = lax.div(place, CORES), lax.rem(place, CORES)
     rows_x = terms.shape[1]
-    rows = out_grad.shape[0]
+    rows = out_states.shape[1]
     tile = rows_x // TILES
 
     def remote(src, dst, ssem, rsem, device):
@@ -190,42 +191,62 @@
     def at_z(i):
         return (rank, i)
 
+    order = [(d, t) for t in range(TILES) for d in range(1, chips_x)]
+    order += [(0, t) for t in range(TILES)]
+
+    def columns(d, t):
+        return pl.ds(pl.multiple_of(lax.rem(x + d, chips_x) * rows_x + t * tile, tile), tile)
+
+    def token_copy(d, t):
+        part = columns(d, t)
+        return pltpu.make_async_copy(tokens_in.at[:, part], tokens.at[:, part], in_sem.at[d, t])
+
     barrier = pltpu.get_barrier_semaphore()
-    for me, count, device in ((x, chips_x, at_x), (place, peers, at_place), (z, shards, at_z)):
+    for me, count, device in ((z, shards, at_z), (x, chips_x, at_x), (place, peers, at_place)):
 
         def greet(d, _, me=me, count=count, device=device):
             pl.semaphore_signal(
-                barrier, inc=1, device_id=device((me + d) % count), device_id_type=MESH
+                barrier, inc=1, device_id=device(lax.rem(me + d, count)), device_id_type=MESH
             )
             return 0
 
         lax.fori_loop(1, count, greet, 0)
 
-    def gradient(owner, t):
-        at = pl.multiple_of(owner * rows_x + t * tile, tile)
+    side = [pltpu.make_async_copy(cotangent_in, cotangent, side_sem.at[0])]
+    for i, ref in enumerate((one_in, two_in, master_in)):
+        side.append(pltpu.make_async_copy(ref, states.at[i], side_sem.at[i + 1]))
+    side[0].start()
+    for d, t in order:
+        token_copy(d, t).start()
+    for copy in side[1:]:
+        copy.start()
+
+    def gradient(d, t):
+        token_copy(d, t).wait()
         return lax.dot_general(
-            tokens[:, pl.ds(at, tile)], cotangent[...], (((0,), (0,)), ((), ())),
+            tokens[:, columns(d, t)], cotangent[...], (((0,), (0,)), ((), ())),
             preferred_element_type=jnp.float32,
         )
 
     def x_copy(d, t):
-        to = (x + d) % chips_x
+        to = lax.rem(x + d, chips_x)
         return remote(
             x_send.at[d - 1, t], x_recv.at[x, t], x_ssem.at[d - 1, t], x_rsem.at[x, t], at_x(to)
         )
 
+    side[0].wait()
+    for d, t in order:
+        if d == 0:
+            terms[x, t * tile : t * tile + tile, :] = gradient(d, t)
+            continue
+        encode(gradient(d, t), x_send.at[d - 1, t])
+        if (d, t) == order[0]:
+            pl.semaphore_wait(barrier, chips_x + peers + shards - 3)
+        x_copy(d, t).start()
+
     for t in range(TILES):
         for d in range(1, chips_x):
-            encode(gradient((x + d) % chips_x, t), x_send.at[d - 1, t])
-            if t == 0 and d == 1:
-                pl.semaphore_wait(barrier, chips_x + peers + shards - 3)
-            x_copy(d, t).start()
-    for t in range(TILES):
-        terms[x, t * tile : t * tile + tile, :] = gradient(x, t)
-
-    for t in range(TILES):
-        for d in range(1, chips_x):
-            source = (x + d) % chips_x
+            source = lax.rem(x + d, chips_x)
             remote(
                 x_send.at[d - 1, t], x_recv.at[source, t],
                 x_ssem.at[d - 1, t], x_rsem.at[source, t], at_x(source),
@@ -243,23 +264,21 @@
             return remote(slots.at[i], slots.at[i], ssem.at[to], rsem.at[i], device(to))
 
         def send(d, _):
-            copy(me, (me + d) % count).start()
+            copy(me, lax.rem(me + d, count)).start()
             return 0
 
         def wait(d, _):
-            other = (me + d) % count
+            other = lax.rem(me + d, count)
             copy(other, other).wait_recv()
             return 0
 
         def done(d, _):
-            copy(me, (me + d) % count).wait_send()
+            copy(me, lax.rem(me + d, count)).wait_send()
             return 0
 
         lax.fori_loop(1, count, send, 0)
         lax.fori_loop(1, count, wait, 0)
-        result = slots[0]
-        for i in range(1, count):
-            result = result + slots[i]
+        result = jnp.sum(slots[...], axis=0)
         lax.fori_loop(1, count, done, 0)
         return result
 
@@ -287,7 +306,7 @@
         )
 
     def y_start(d, _):
-        to = (place + d) % peers
+        to = lax.rem(place + d, peers)
         encode(y_block(to), y_send.at[to])
         y_copy(to).start()
         return 0
@@ -296,7 +315,7 @@
     parts[place] = y_block(place)
 
     def y_wait(d, _):
-        source = (place + d) % peers
+        source = lax.rem(place + d, peers)
         remote(
             y_send.at[source], y_recv.at[source],
             y_ssem.at[source], y_rsem.at[source], at_place(source),
@@ -313,63 +332,109 @@
     gram = total(gram, y_two, y2_ssem, y2_rsem, place, peers, at_place)
     weight = adasum_weights(unpack(gram, peers), peers)
 
+    for copy in side[1:]:
+        copy.wait()
     for half in range(2):
         lanes = pl.ds(half * 128, 128)
         merged = combine(parts, 0, rows, weight, peers, half)
-        new_one = 0.9 * moment_one[:, lanes] + 0.1 * merged
-        new_two = 0.999 * moment_two[:, lanes] + 0.001 * merged * merged
+        new_one = 0.9 * states[0, :, lanes] + 0.1 * merged
+        new_two = 0.999 * states[1, :, lanes] + 0.001 * merged * merged
         first_fix = 1.0 - 0.9**STEP
         second_fix = 1.0 - 0.999**STEP
-        old = master[:, lanes]
+        old = states[2, :, lanes]
         update = new_one / first_fix / (jnp.sqrt(new_two / second_fix) + 1e-08) + 0.1 * old
         new_master = old - 0.001 * update
-        out_grad[:, lanes] = merged
-        out_one[:, lanes] = new_one
-        out_two[:, lanes] = new_two
-        out_master[:, lanes] = new_master
+        out_states[0, :, lanes] = merged
+        out_states[1, :, lanes] = new_one
+        out_states[2, :, lanes] = new_two
+        out_states[3, :, lanes] = new_master
         out_weights[x, y, core, :, lanes] = new_master.astype(jnp.bfloat16)
 
-    def wy_copy(source, to):
-        block = out_weights.at[x, source, core]
-        return remote(
-            block, block, wy_ssem.at[to], wy_rsem.at[source], (x * peers + to * CORES + core, z)
-        )
-
-    def wx_copy(source, to):
-        block = out_weights.at[source, :, core]
-        return remote(block, block, wx_ssem.at[to], wx_rsem.at[source], at_x(to))
-
-    def wc_copy(source, which):
-        block = out_weights.at[source, :, which]
-        return remote(
-            block, block, wc_ssem.at[source], wc_rsem.at[source], at_place(y * CORES + 1 - core)
-        )
-
-    for d in range(1, chips_y):
-        wy_copy(y, (y + d) % chips_y).start()
-    for d in range(1, chips_y):
-        wy_copy((y + d) % chips_y, (y + d) % chips_y).wait_recv()
-    for d in range(1, chips_x):
-        wx_copy(x, (x + d) % chips_x).start()
-    wc_copy(x, core).start()
-    for d in range(1, chips_x):
-        source = (x + d) % chips_x
-        wx_copy(source, source).wait_recv()
-        wc_copy(source, core).start()
-    for i in range(chips_x):
-        wc_copy(i, 1 - core).wait_recv()
-    for i in range(chips_x):
-        wc_copy(i, core).wait_send()
-    for d in range(1, chips_x):
-        wx_copy(x, (x + d) % chips_x).wait_send()
-    for d in range(1, chips_y):
-        wy_copy(y, (y + d) % chips_y).wait_send()
+    class Stream:
+        def __init__(self, index, start, size, swapped):
+            self.index, self.part, self.swapped = index, pl.ds(start, size), swapped
+            self.count = (chips_x, chips_y) if swapped else (chips_y, chips_x)
+            self.me = (x, y) if swapped else (y, x)
+
+        def block(self, i, j, which):
+            i, j = (i, j) if self.swapped else (j, i)
+            return out_weights.at[i, j, which, self.part]
+
+        def device(self, i, j):
+            i, j = (i, j) if self.swapped else (j, i)
+            return (i * peers + j * CORES + core, z)
+
+        def a(self, source, to):
+            block = self.block(source, self.me[1], core)
+            return remote(
+                block, block, wa_ssem.at[self.index, to], wa_rsem.at[self.index, source],
+                self.device(to, self.me[1]),
+            )
+
+        def b(self, first, second, to):
+            block = self.block(first, second, core)
+            return remote(
+                block, block, wb_ssem.at[self.index, first, to],
+                wb_rsem.at[self.index, first, second], self.device(self.me[0], to),
+            )
+
+        def c(self, first, second, which):
+            block = self.block(first, second, which)
+            return remote(
+                block, block, wc_ssem.at[self.index, first, second],
+                wc_rsem.at[self.index, first, second], at_place(y * CORES + 1 - core),
+            )
+
+        def others(self, axis):
+            count = self.count[axis]
+            near = sorted(range(1, count), key=lambda d: min(d, count - d))
+            return [lax.rem(self.me[axis] + d, count) for d in near]
+
+        def forward(self, first):
+            for to in self.others(1):
+                self.b(first, self.me[1], to).start()
+            self.c(first, self.me[1], core).start()
+
+        def start(self):
+            for to in self.others(0):
+                self.a(self.me[0], to).start()
+            self.forward(self.me[0])
+
+        def middle(self):
+            for source in self.others(0):
+                self.a(source, source).wait_recv()
+                self.forward(source)
+
+        def last(self):
+            for second in self.others(1):
+                for first in [self.me[0]] + self.others(0):
+                    self.b(first, second, second).wait_recv()
+                    self.c(first, second, core).start()
+
+        def finish(self):
+            for first in [self.me[0]] + self.others(0):
+                for second in [self.me[1]] + self.others(1):
+                    self.c(first, second, 1 - core).wait_recv()
+                    self.c(first, second, core).wait_send()
+                for to in self.others(1):
+                    self.b(first, self.me[1], to).wait_send()
+            for to in self.others(0):
+                self.a(self.me[0], to).wait_send()
+
+    first_rows = rows * 3 // 4 // 16 * 16
+    streams = [Stream(0, 0, first_rows, False)]
+    if rows > first_rows:
+        streams.append(Stream(1, first_rows, rows - first_rows, True))
+    for stage in ("start", "middle", "last", "finish"):
+        for stream in streams[:: -1 if stage == "middle" else 1]:
+            getattr(stream, stage)()
+
     for d in range(1, chips_x):
         for t in range(TILES):
             x_copy(d, t).wait_send()
 
     def y_done(d, _):
-        y_copy((place + d) % peers).wait_send()
+        y_copy(lax.rem(place + d, peers)).wait_send()
         return 0
 
     lax.fori_loop(1, peers, y_done, 0)
@@ -388,17 +453,22 @@
     one = (packing(chips_x)[1], 128)
     two = (packing(peers)[1], 128)
     dma = pltpu.SemaphoreType.DMA
-    block = jax.ShapeDtypeStruct((rows, wide), f32)
+    most = max(chips_x, chips_y)
+    anywhere = pl.BlockSpec(memory_space=pl.ANY)
     vmem = pl.BlockSpec(memory_space=pltpu.VMEM)
-    outs = pl.pallas_call(
+    states, weights = pl.pallas_call(
         functools.partial(kernel, chips_x, shards),
         out_shape=(
-            block, block, block, block,
+            jax.ShapeDtypeStruct((4, rows, wide), f32),
             jax.ShapeDtypeStruct((chips_x, chips_y, CORES, rows, wide), jnp.bfloat16),
         ),
-        in_specs=[vmem] * 5,
-        out_specs=(vmem,) * 5,
+        in_specs=[anywhere] * 5,
+        out_specs=(vmem,) * 2,
         scratch_shapes=[
+            pltpu.VMEM(tokens.shape, jnp.bfloat16),
+            pltpu.VMEM(cotangent.shape, jnp.bfloat16),
+            pltpu.VMEM((3, rows, wide), f32),
+            dma((chips_x, TILES)), dma((4,)),
             pltpu.VMEM((chips_x - 1, TILES, 2 * tile + HEAD, 128), coded),
             pltpu.VMEM((chips_x, TILES, 2 * tile + HEAD, 128), coded),
             pltpu.VMEM((chips_x, rows_x, wide), f32),
@@ -419,12 +489,12 @@
             dma((shards,)), dma((shards,)),
             dma((chips_x,)), dma((chips_x,)),
             dma((peers,)), dma((peers,)),
-            dma((chips_y,)), dma((chips_y,)),
-            dma((chips_x,)), dma((chips_x,)),
-            dma((chips_x,)), dma((chips_x,)),
+            dma((2, most)), dma((2, most)),
+            dma((2, most, most)), dma((2, most, most)),
+            dma((2, most, most)), dma((2, most, most)),
         ],
         compiler_params=pltpu.CompilerParams(
-            collective_id=0, has_side_effects=True, vmem_limit_bytes=48 * 1024 * 1024
+            collective_id=0, has_side_effects=True, vmem_limit_bytes=60 * 1024 * 1024
         ),
         cost_estimate=pl.CostEstimate(
             flops=2 * tokens.shape[0] * depth * wide,
@@ -432,7 +502,24 @@
             transcendentals=0,
         ),
     )(tokens, cotangent, moment_one, moment_two, master)
-    return outs[:4] + (outs[4].reshape(depth, wide),)
+    block = jax.ShapeDtypeStruct((rows, wide), f32)
+    return pl.pallas_call(
+        hand_out,
+        out_shape=(block,) * 4 + (jax.ShapeDtypeStruct((depth, wide), jnp.bfloat16),),
+        in_specs=[vmem] * 2,
+        out_specs=(anywhere,) * 5,
+        scratch_shapes=[dma((5,))],
+    )(states, weights.reshape(depth, wide))
+
+
+def hand_out(states, weights, *refs):
+    outs, sem = refs[:5], refs[5]
+    copies = [pltpu.make_async_copy(states.at[i], outs[i], sem.at[i]) for i in range(4)]
+    copies.insert(0, pltpu.make_async_copy(weights, outs[4], sem.at[4]))
+    for copy in copies:
+        copy.start()
+    for copy in copies:
+        copy.wait()
 
 
 def solution(mesh, chips_y=CHIPS_Y):

time: 129 us -> 119 us (0.922)
  local copies, waits for them, and re-layouts: 9.16 us -> 0 us
    unnamed x15 -> x0, local copies, waits for them, and re-layouts: 9.16 us -> none
    pallas_call x1 -> x2, Pallas kernels: 119 us -> 118 us  [the longest x1 115 us: body(): pl.pallas_call(functools.partial(kernel, chips_x, shards), out_shape=(jax...]
where the time goes in v2:
time: 119 us
  Pallas kernels  118 us (99%)
    pallas_call x1, Pallas kernels, body(): pl.pallas_call(functools.partial(kernel, chips_x, shards), out_shape=(jax...  115 us
    pallas_call x1, Pallas kernels, body(): pl.pallas_call(hand_out, out_shape=(block,) * 4 + (jax.ShapeDtypeStruct((...  3.12 us

profile of v2, /device:TPU:1, one launch (start us, length us, event | category | flops | bytes accessed | tf_op | source)
XLA Modules:
  0.0 118.9 jit_solution(13479954722425483529)
XLA Ops:
  0.6 115.2 %shard_map.92 = (f32[4,64,256]{2,1,0:T(8,128)}, bf16[4,8,2,64,256]{4,3,2,1,0:T(8,128)(2,1)}) custom-call(bf16[384,4096]{1,0:T(8,128)(2,1)} %tokens_in.1, bf16[384,256]{1,0:T(8,128)(2,1)} %cotangent_in.1, f32[64,256]{1,0:T(8,128)} %one_in.1, f32[64,256]{1,0:T(8,128)} %two_in.1, f32[64,256]{1,0:T(8,128)} %master_in.1), custom_call_target="tpu_custom_call" | custom-call | flops 805306368 | bytes 6291456 | tf_op jit(solution)/shard_map/pallas_call | solution.py:459
  115.8 3.1 %shard_map.93 = (f32[64,256]{1,0:T(8,128)}, f32[64,256]{1,0:T(8,128)}, f32[64,256]{1,0:T(8,128)}, f32[64,256]{1,0:T(8,128)}, bf16[4096,256]{1,0:T(8,128)(2,1)}) custom-call(f32[4,64,256]{2,1,0:T(8,128)} %get-tuple-element.7.states, bf16[4096,256]{1,0:T(8,128)(2,1)} %bitcast.1), custom_call_target="tpu_custom_call" | custom-call | tf_op jit(solution)/shard_map/pallas_call | solution.py:506

commit v3 on v2

--- a/solution.py
+++ b/solution.py
@@ -163,6 +163,7 @@
     tokens, cotangent, states, in_sem, side_sem,
     x_send, x_recv, terms, x_sums, y_send, y_recv, parts, y_sums,
     z_one, x_one, z_two, x_two, y_two,
+    raw_send, raw_recv, factors, raw_ssem, raw_rsem, f_ssem, f_rsem,
     x_ssem, x_rsem, y_ssem, y_rsem,
     z1_ssem, z1_rsem, x1_ssem, x1_rsem, z2_ssem, z2_rsem, x2_ssem, x2_rsem, y2_ssem, y2_rsem,
     wa_ssem, wa_rsem, wb_ssem, wb_rsem, wc_ssem, wc_rsem,
@@ -175,6 +176,12 @@
     rows_x = terms.shape[1]
     rows = out_states.shape[1]
     tile = rows_x // TILES
+    per_tile = peers // TILES
+    early = rows // 4
+    late = rows - early
+
+    def tile_of(t):
+        return lax.rem(lax.div(place, per_tile) + t + core * (TILES - 2 * t), TILES)
 
     def remote(src, dst, ssem, rsem, device):
         return pltpu.make_async_remote_copy(
@@ -195,7 +202,7 @@
     order += [(0, t) for t in range(TILES)]
 
     def columns(d, t):
-        return pl.ds(pl.multiple_of(lax.rem(x + d, chips_x) * rows_x + t * tile, tile), tile)
+        return pl.ds(pl.multiple_of(lax.rem(x + d, chips_x) * rows_x + tile_of(t) * tile, tile), tile)
 
     def token_copy(d, t):
         part = columns(d, t)
@@ -237,14 +244,26 @@
     side[0].wait()
     for d, t in order:
         if d == 0:
-            terms[x, t * tile : t * tile + tile, :] = gradient(d, t)
+            terms[x, pl.ds(pl.multiple_of(tile_of(t) * tile, tile), tile), :] = gradient(d, t)
             continue
         encode(gradient(d, t), x_send.at[d - 1, t])
         if (d, t) == order[0]:
             pl.semaphore_wait(barrier, chips_x + peers + shards - 3)
         x_copy(d, t).start()
 
+    def raw_copy(to):
+        return remote(
+            raw_send.at[to], raw_recv.at[place], raw_ssem.at[to], raw_rsem.at[place], at_place(to)
+        )
+
+    def raw_start(to):
+        at = pl.ds(pl.multiple_of(to * rows, rows), early)
+        block = jnp.concatenate([terms[k, at, :] for k in range(chips_x)], axis=0)
+        encode(block, raw_send.at[to])
+        raw_copy(to).start()
+
     for t in range(TILES):
+        part = pl.ds(pl.multiple_of(tile_of(t) * tile, tile), tile)
         for d in range(1, chips_x):
             source = lax.rem(x + d, chips_x)
             remote(
@@ -252,10 +271,24 @@
                 x_ssem.at[d - 1, t], x_rsem.at[source, t], at_x(source),
             ).wait_recv()
             for half in range(2):
-                terms[source, t * tile : t * tile + tile, half * 128 : half * 128 + 128] = decode(
+                terms[source, part, half * 128 : half * 128 + 128] = decode(
                     x_recv.at[source, t], tile, half
                 )
-        pair_sums(terms.at[:, pl.ds(t * tile, tile), :], x_sums, chips_x, tile, t == 0)
+        if t == TILES - 1:
+            pair_sums(terms.at[:, part, :], x_sums, chips_x, tile, False)
+
+        def raw_step(j, _, t=t):
+            to = tile_of(t) * per_tile + j
+
+            @pl.when(to != place)
+            def _():
+                raw_start(to)
+
+            return 0
+
+        lax.fori_loop(0, per_tile, raw_step, 0)
+        if t < TILES - 1:
+            pair_sums(terms.at[:, part, :], x_sums, chips_x, tile, t == 0)
 
     def total(value, slots, ssem, rsem, me, count, device):
         slots[me] = value
@@ -299,20 +332,54 @@
             y_send.at[to], y_recv.at[place], y_ssem.at[to], y_rsem.at[place], at_place(to)
         )
 
-    def y_block(to):
-        at = pl.multiple_of(to * rows, rows)
+    def f_copy(to):
+        return remote(
+            factors.at[place], factors.at[place], f_ssem.at[to], f_rsem.at[place], at_place(to)
+        )
+
+    factors[place] = weight[:chips_x, :]
+
+    def f_start(d, _):
+        f_copy(lax.rem(place + d, peers)).start()
+        return 0
+
+    lax.fori_loop(1, peers, f_start, 0)
+
+    def y_block(to, first, size):
+        at = pl.multiple_of(to * rows + first, 16)
         return jnp.concatenate(
-            [combine(terms, at, rows, weight, chips_x, half) for half in range(2)], axis=1
+            [combine(terms, at, size, weight, chips_x, half) for half in range(2)], axis=1
         )
 
     def y_start(d, _):
         to = lax.rem(place + d, peers)
-        encode(y_block(to), y_send.at[to])
+        encode(y_block(to, early, late), y_send.at[to])
         y_copy(to).start()
         return 0
 
     lax.fori_loop(1, peers, y_start, 0)
-    parts[place] = y_block(place)
+    parts[place] = y_block(place, 0, rows)
+
+    def raw_wait(d, _):
+        source = lax.rem(place + d, peers)
+        remote(
+            raw_send.at[source], raw_recv.at[source],
+            raw_ssem.at[source], raw_rsem.at[source], at_place(source),
+        ).wait_recv()
+        remote(
+            factors.at[source], factors.at[source],
+            f_ssem.at[source], f_rsem.at[source], at_place(source),
+        ).wait_recv()
+        factor = factors[source]
+        for half in range(2):
+            value = decode(raw_recv.at[source], chips_x * early, half)
+            mix = factor[0:1, :] * value[:early, :]
+            for k in range(1, chips_x):
+                mix = mix + factor[k : k + 1, :] * value[k * early : k * early + early, :]
+            parts[source, :early, half * 128 : half * 128 + 128] = mix
+        return 0
+
+    lax.fori_loop(1, peers, raw_wait, 0)
 
     def y_wait(d, _):
         source = lax.rem(place + d, peers)
@@ -321,7 +388,9 @@
             y_ssem.at[source], y_rsem.at[source], at_place(source),
         ).wait_recv()
         for half in range(2):
-            parts[source, :, pl.ds(half * 128, 128)] = decode(y_recv.at[source], rows, half)
+            parts[source, early:, half * 128 : half * 128 + 128] = decode(
+                y_recv.at[source], late, half
+            )
         return 0
 
     lax.fori_loop(1, peers, y_wait, 0)
@@ -434,7 +503,10 @@
             x_copy(d, t).wait_send()
 
     def y_done(d, _):
-        y_copy(lax.rem(place + d, peers)).wait_send()
+        to = lax.rem(place + d, peers)
+        y_copy(to).wait_send()
+        raw_copy(to).wait_send()
+        f_copy(to).wait_send()
         return 0
 
     lax.fori_loop(1, peers, y_done, 0)
@@ -448,6 +520,8 @@
     depth, wide = tokens.shape[1], cotangent.shape[1]
     rows_x, rows = depth // chips_x, depth // ranks
     tile = rows_x // TILES
+    early = rows // 4
+    late = rows - early
     coded = jnp.bfloat16
     f32 = jnp.float32
     one = (packing(chips_x)[1], 128)
@@ -473,8 +547,8 @@
             pltpu.VMEM((chips_x, TILES, 2 * tile + HEAD, 128), coded),
             pltpu.VMEM((chips_x, rows_x, wide), f32),
             pltpu.VMEM((chips_x * max(chips_x, 8) * 8, 128), f32),
-            pltpu.VMEM((peers, 2 * rows + HEAD, 128), coded),
-            pltpu.VMEM((peers, 2 * rows + HEAD, 128), coded),
+            pltpu.VMEM((peers, 2 * late + HEAD, 128), coded),
+            pltpu.VMEM((peers, 2 * late + HEAD, 128), coded),
             pltpu.VMEM((peers, rows, wide), f32),
             pltpu.VMEM((peers * max(peers, 8) * 8, 128), f32),
             pltpu.VMEM((shards,) + one, f32),
@@ -482,6 +556,10 @@
             pltpu.VMEM((shards,) + two, f32),
             pltpu.VMEM((chips_x,) + two, f32),
             pltpu.VMEM((peers,) + two, f32),
+            pltpu.VMEM((peers, 2 * chips_x * early + HEAD, 128), coded),
+            pltpu.VMEM((peers, 2 * chips_x * early + HEAD, 128), coded),
+            pltpu.VMEM((peers, chips_x, 128), f32),
+            dma((peers,)), dma((peers,)), dma((peers,)), dma((peers,)),
             dma((chips_x - 1, TILES)), dma((chips_x, TILES)),
             dma((peers,)), dma((peers,)),
             dma((shards,)), dma((shards,)),

time: 119 us -> 118 us (level)
  no operation moved by 1% of the time
where the time goes in v3:
time: 118 us
  Pallas kernels  117 us (99%)
    pallas_call x1, Pallas kernels, body(): pl.pallas_call(functools.partial(kernel, chips_x, shards), out_shape=(jax...  114 us
    pallas_call x1, Pallas kernels, body(): pl.pallas_call(hand_out, out_shape=(block,) * 4 + (jax.ShapeDtypeStruct((...  3.12 us

profile of v3, /device:TPU:1, one launch (start us, length us, event | category | flops | bytes accessed | tf_op | source)
XLA Modules:
  0.0 117.9 jit_solution(9386326294384760187)
XLA Ops:
  0.6 114.1 %shard_map.92 = (f32[4,64,256]{2,1,0:T(8,128)}, bf16[4,8,2,64,256]{4,3,2,1,0:T(8,128)(2,1)}) custom-call(bf16[384,4096]{1,0:T(8,128)(2,1)} %tokens_in.1, bf16[384,256]{1,0:T(8,128)(2,1)} %cotangent_in.1, f32[64,256]{1,0:T(8,128)} %one_in.1, f32[64,256]{1,0:T(8,128)} %two_in.1, f32[64,256]{1,0:T(8,128)} %master_in.1), custom_call_target="tpu_custom_call" | custom-call | flops 805306368 | bytes 6291456 | tf_op jit(solution)/shard_map/pallas_call | solution.py:533
  114.8 3.1 %shard_map.93 = (f32[64,256]{1,0:T(8,128)}, f32[64,256]{1,0:T(8,128)}, f32[64,256]{1,0:T(8,128)}, f32[64,256]{1,0:T(8,128)}, bf16[4096,256]{1,0:T(8,128)(2,1)}) custom-call(f32[4,64,256]{2,1,0:T(8,128)} %get-tuple-element.7.states, bf16[4096,256]{1,0:T(8,128)(2,1)} %bitcast.1), custom_call_target="tpu_custom_call" | custom-call | tf_op jit(solution)/shard_map/pallas_call | solution.py:584
